TPU v7x, 32 devices: a whole 2x2x4 slice. The times are simulated.
32 devices in a mesh: groups: 2 (over x), row: 16 (over z, y, core).
Axes of the slice: x: 2, y: 2, z: 4, core: 2. Of those that a mesh axis runs over, the one named last changes fastest.
Arguments:
- source_features: bfloat16 [32768, 64], P(('groups', 'row')), parts along dimension 0, may hold values from -80 to 80
- target_features: bfloat16 [262144, 64], P('groups'), parts along dimension 0, may hold values from -4 to 4
- source_weights: float32 [32768], P(('groups', 'row')), parts along dimension 0, may hold values from -1 to 1
- target_weights: float32 [262144], P('groups'), parts along dimension 0, may hold values from -1 to 1
- block_columns: int32 [128, 32], P(('groups', 'row')), parts along dimension 0, may hold values from 0 to 511, as said below
- block_counts: int32 [128], P(('groups', 'row')), parts along dimension 0, may hold values from 8 to 32
Outputs:
- source_potential: float32 [32768], P(('groups', 'row')), parts along dimension 0
- target_potential: float32 [262144], P(('groups', 'row')), parts along dimension 0
There are 2 independent parts, one for each index of `groups`. A program takes and returns all parts, laid end to end along the dimension named above; each array names one. Nothing has to cross between parts.
Inputs may be any that keep to these rules, and one draw needn't show every extreme that they name: `block_columns`: the 32 entries of a row are distinct; every target block is named among the first block_counts[p] entries of some row p; entries from block_counts[p] on are not part of the support.
All inputs are finite; a program needn't handle non-finite values.
Results may differ from a plain program's by a relative error of at most 0.0003.
Values sent between devices are 32-bit elements; how exact they have to be, the bound alone decides.
A program may use at most 128 MiB of HBM per device.

v0:
```python
import jax
import jax.numpy as jnp
from jax import lax
from jax.sharding import PartitionSpec as P

BLOCK = 256
ITERS = 3


EPSILON = 1.0
FLOOR = -1e30


def local(
    source_features, target_features, source_weights, target_weights, block_columns, block_counts
):
    own_blocks = block_columns.shape[0]
    slots = block_columns.shape[1]
    target_count = target_features.shape[0] // BLOCK
    width = target_features.shape[1]
    source_blocks = source_features.reshape(own_blocks, BLOCK, width)
    target_blocks = target_features.reshape(target_count, BLOCK, width)
    weights_src = source_weights.reshape(own_blocks, BLOCK)
    weights_tgt = target_weights.reshape(target_count, BLOCK)
    usable = jnp.arange(slots, dtype=jnp.int32)[None, :] < block_counts[:, None]
    devices = lax.axis_size("row")
    share = target_count // devices
    position = lax.axis_index("row")

    def block_scores(which):
        columns = block_columns[which]
        picked = target_blocks[columns].reshape(slots * BLOCK, width)
        product = lax.dot_general(
            source_blocks[which],
            picked,
            (((1,), (1,)), ((), ())),
            preferred_element_type=jnp.float32,
        )
        return (product.reshape(BLOCK, slots, BLOCK) / EPSILON, columns)

    source_pot = jnp.zeros((own_blocks, BLOCK), jnp.float32)
    own_pot = jnp.zeros((share, BLOCK), jnp.float32)
    for sweep in range(ITERS):

        def column_step(which, carry):
            running_max, running_sum = carry
            scores, columns = block_scores(which)
            scores = scores + source_pot[which][:, None, None]
            block_max = jnp.max(scores, axis=0)
            block_sum = jnp.sum(jnp.exp(scores - block_max[None]), axis=0)
            keep = usable[which][:, None]
            block_max = jnp.where(keep, block_max, FLOOR)
            block_sum = jnp.where(keep, block_sum, 0.0)
            old_max = running_max[columns]
            old_sum = running_sum[columns]
            new_max = jnp.maximum(old_max, block_max)
            new_sum = old_sum * jnp.exp(old_max - new_max) + block_sum * jnp.exp(
                block_max - new_max
            )
            return (running_max.at[columns].set(new_max), running_sum.at[columns].set(new_sum))

        start = (
            jnp.full((target_count, BLOCK), FLOOR, jnp.float32),
            jnp.zeros((target_count, BLOCK), jnp.float32),
        )
        running_max, running_sum = lax.fori_loop(0, own_blocks, column_step, start)
        global_max = lax.pmax(running_max, "row")
        scaled = running_sum * jnp.exp(running_max - global_max)
        summed = lax.psum(scaled, "row")
        target_pot = weights_tgt - (global_max + jnp.log(summed))
        own_pot = lax.dynamic_slice_in_dim(target_pot, position * share, share, 0)

        def row_step(which):
            scores, columns = block_scores(which)
            scores = scores + target_pot[columns][None]
            scores = jnp.where(usable[which][None, :, None], scores, FLOOR)
            top = jnp.max(scores, axis=(1, 2))
            summed_row = jnp.sum(jnp.exp(scores - top[:, None, None]), axis=(1, 2))
            return weights_src[which] - (top + jnp.log(summed_row))

        source_pot = lax.map(row_step, jnp.arange(own_blocks, dtype=jnp.int32))
    return (source_pot.reshape(-1), own_pot.reshape(-1))


def solution(mesh):
    return jax.shard_map(
        local,
        mesh=mesh,
        in_specs=(
            P(("groups", "row"), None),
            P("groups", None),
            P(("groups", "row")),
            P("groups"),
            P(("groups", "row"), None),
            P(("groups", "row")),
        ),
        out_specs=(P(("groups", "row")), P(("groups", "row"))),
        check_vma=False,
    )
```

profile of v0, /device:TPU:0, one launch (start us, length us, event | category | flops | bytes accessed | tf_op | source)
XLA Modules:
  0.0 822.9 jit_solution(14022748329216579938)
XLA Ops:
  7.2 30.0 %copy.21 = bf16[131072,64]{1,0:T(8,128)(2,1)} copy(bf16[131072,64]{0,1:T(8,128)(2,1)} %param.19) | data formatting | bytes 33554432 | tf_op args[1]
  37.5 32.2 %while.75 = (s32[]{:T(128)}, f32[512,256]{1,0:T(8,128)S(1)}, f32[512,256]{1,0:T(8,128)S(1)}, s32[4,32]{1,0:T(4,128)S(1)}, pred[4,32]{1,0:T(4,128)(4,1)S(1)}, /*i...) while((s32[]{:T(128)}, f32[512,256]{1,0:T(8,128)S(1)}, ...), condition=%wide.region_5.6_spmd, body=%wide.region_0.5_spmd.sunk | while | flops 274793568 | bytes 22914876 | solution.py:66
  37.5 2.4 gather_fusion.1
  45.6 2.4 gather_fusion.1
  53.6 2.4 gather_fusion.1
  61.7 2.4 gather_fusion.1
  70.6 93.2 %all-reduce.7.cloned.1.call-done = f32[512,256]{1,0:T(8,128)} async-done(((f32[512,256]{1,0:T(8,128)}), f32[512,256]{1,0:T(8,128)}) %all-reduce.7.cloned.1.call-update) | async-done | bytes 524304 | tf_op jit(solution)/shard_map/pmax | solution.py:67
  167.3 90.8 %all-reduce.9.cloned.1.call-done = f32[512,256]{1,0:T(8,128)} async-done(((f32[512,256]{1,0:T(8,128)}), f32[512,256]{1,0:T(8,128)}) %all-reduce.9.cloned.1.call-update) | async-done | bytes 524304 | tf_op jit(solution)/shard_map/psum | solution.py:69
  259.5 37.8 %while.76 = (s32[]{:T(128)}, f32[4,256]{1,0:T(4,128)S(1)}, s32[4]{0:T(128)S(1)}, f32[4,256]{1,0:T(4,128)S(1)}, pred[4,32]{1,0:T(4,128)(4,1)S(1)}, /*index=5*/bf1...) while((s32[]{:T(128)}, f32[4,256]{1,0:T(4,128)S(1)}, ...), condition=%wide.region_11.12_spmd, body=%wide.region_8.11_spmd.sunk | while | flops 283116640 | bytes 21152152 | solution.py:81
  262.9 2.4 gather_fusion.3
  266.7 2.2 exponential_reduce_fusion.13
  272.3 2.4 gather_fusion.3
  276.2 2.2 exponential_reduce_fusion.13
  281.8 2.4 gather_fusion.3
  285.6 2.2 exponential_reduce_fusion.13
  291.2 2.4 gather_fusion.3
  295.1 2.2 exponential_reduce_fusion.13
  297.4 33.5 %while.77 = (s32[]{:T(128)}, f32[512,256]{1,0:T(8,128)S(1)}, f32[512,256]{1,0:T(8,128)S(1)}, s32[4,32]{1,0:T(4,128)S(1)}, pred[4,32]{1,0:T(4,128)(4,1)S(1)}, /*i...) while((s32[]{:T(128)}, f32[512,256]{1,0:T(8,128)S(1)}, ...), condition=%wide.region_17.18_spmd, body=%wide.region_12.17_spmd.sunk | while | flops 278987872 | bytes 22918984 | solution.py:66
  297.4 2.4 gather_fusion.5
  305.8 2.4 gather_fusion.5
  314.2 2.4 gather_fusion.5
  322.6 2.4 gather_fusion.5
  331.8 91.0 %all-reduce.11.cloned.1.call-done = f32[512,256]{1,0:T(8,128)} async-done(((f32[512,256]{1,0:T(8,128)}), f32[512,256]{1,0:T(8,128)}) %all-reduce.11.cloned.1.call-update) | async-done | bytes 524304 | tf_op jit(solution)/shard_map/pmax | solution.py:67
  425.2 91.5 %all-reduce.13.cloned.1.call-done = f32[512,256]{1,0:T(8,128)} async-done(((f32[512,256]{1,0:T(8,128)}), f32[512,256]{1,0:T(8,128)}) %all-reduce.13.cloned.1.call-update) | async-done | bytes 524304 | tf_op jit(solution)/shard_map/psum | solution.py:69
  518.2 37.8 %while.78 = (s32[]{:T(128)}, f32[4,256]{1,0:T(4,128)S(1)}, s32[4]{0:T(128)S(1)}, f32[4,256]{1,0:T(4,128)S(1)}, pred[4,32]{1,0:T(4,128)(4,1)S(1)}, /*index=5*/bf1...) while((s32[]{:T(128)}, f32[4,256]{1,0:T(4,128)S(1)}, ...), condition=%wide.region_23.24_spmd, body=%wide.region_20.23_spmd.sunk | while | flops 283116640 | bytes 21152152 | solution.py:81
  521.6 2.4 gather_fusion.7
  525.4 2.1 exponential_reduce_fusion.15
  531.0 2.4 gather_fusion.7
  534.9 2.1 exponential_reduce_fusion.15
  540.5 2.4 gather_fusion.7
  544.3 2.1 exponential_reduce_fusion.15
  549.9 2.4 gather_fusion.7
  553.8 2.1 exponential_reduce_fusion.15
  556.1 33.5 %while.79 = (s32[]{:T(128)}, f32[512,256]{1,0:T(8,128)S(1)}, f32[512,256]{1,0:T(8,128)S(1)}, s32[4,32]{1,0:T(4,128)S(1)}, pred[4,32]{1,0:T(4,128)(4,1)S(1)}, /*i...) while((s32[]{:T(128)}, f32[512,256]{1,0:T(8,128)S(1)}, ...), condition=%wide.region_29.30_spmd, body=%wide.region_24.29_spmd.sunk | while | flops 278987872 | bytes 22918984 | solution.py:66
  556.1 2.4 gather_fusion.9
  564.5 2.4 gather_fusion.9
  572.9 2.4 gather_fusion.9
  581.3 2.4 gather_fusion.9
  590.5 91.0 %all-reduce.15.cloned.1.call-done = f32[512,256]{1,0:T(8,128)} async-done(((f32[512,256]{1,0:T(8,128)}), f32[512,256]{1,0:T(8,128)}) %all-reduce.15.cloned.1.call-update) | async-done | bytes 524304 | tf_op jit(solution)/shard_map/pmax | solution.py:67
  683.6 92.2 %all-reduce.17.cloned.1.call-done = f32[512,256]{1,0:T(8,128)} async-done(((f32[512,256]{1,0:T(8,128)}), f32[512,256]{1,0:T(8,128)}) %all-reduce.17.cloned.1.call-update) | async-done | bytes 524304 | tf_op jit(solution)/shard_map/psum | solution.py:69
  777.9 37.5 %while.80 = (s32[]{:T(128)}, f32[4,256]{1,0:T(4,128)S(1)}, s32[4]{0:T(128)S(1)}, f32[4,256]{1,0:T(4,128)S(1)}, pred[4,32]{1,0:T(4,128)(4,1)S(1)}, /*index=5*/bf1...) while((s32[]{:T(128)}, f32[4,256]{1,0:T(4,128)S(1)}, ...), condition=%wide.region_35.36_spmd, body=%wide.region_32.35_spmd.sunk | while | flops 283116640 | bytes 21152152 | solution.py:81
  781.2 2.4 gather_fusion.11
  785.0 2.1 exponential_reduce_fusion.17
  790.6 2.4 gather_fusion.11
  794.4 2.1 exponential_reduce_fusion.17
  800.0 2.4 gather_fusion.11
  803.8 2.1 exponential_reduce_fusion.17
  809.4 2.4 gather_fusion.11
  (266 shorter events, 122.2 us)
Async XLA Ops:
  7.2 30.1 %copy-start.4 = (bf16[1024,64]{0,1:T(8,128)(2,1)S(1)}, bf16[1024,64]{0,1:T(8,128)(2,1)}, u32[]{:S(2)}) copy-start(bf16[1024,64]{0,1:T(8,128)(2,1)} %param.18) | copy-start | bytes 393220
  7.2 30.1 %copy-start.7 = (s32[4]{0:T(128)S(1)}, s32[4]{0:T(128)}, u32[]{:S(2)}) copy-start(s32[4]{0:T(128)} %param.23) | copy-start | bytes 52
  7.2 30.3 %copy-start.6 = (s32[4,32]{1,0:T(4,128)S(1)}, s32[4,32]{1,0:T(4,128)}, u32[]{:S(2)}) copy-start(s32[4,32]{1,0:T(4,128)} %param.22) | copy-start | bytes 1540
  7.2 156.5 %all-reduce.7.cloned.1.call-start = ((), (), s32[]{:S(2)}) async-start(), calls=%async_computation | async-start | bytes 1048576 | tf_op jit(solution)/shard_map/pmax | solution.py:67
  37.5 129.8 %copy-start.5 = (f32[1024]{0:T(1024)S(1)}, f32[1024]{0:T(1024)}, u32[]{:S(2)}) copy-start(f32[1024]{0:T(1024)} %param.20) | copy-start | bytes 12292
  69.7 0.8 copy-start
  70.5 187.6 %all-reduce.9.cloned.1.call-start = ((), (), s32[]{:S(2)}) async-start(), calls=%async_computation.1 | async-start | bytes 1048576 | tf_op jit(solution)/shard_map/psum | solution.py:69
  165.9 256.9 %all-reduce.11.cloned.1.call-start = ((), (), s32[]{:S(2)}) async-start(), calls=%async_computation.2 | async-start | bytes 1048576 | tf_op jit(solution)/shard_map/pmax | solution.py:67
  167.3 92.2 %copy-start.3 = (f32[512,256]{1,0:T(8,128)}, f32[512,256]{1,0:T(8,128)S(1)}, u32[]{:S(2)}) copy-start(f32[512,256]{1,0:T(8,128)S(1)} %reshape.301) | copy-start | bytes 1572868
  330.9 0.8 copy-start.1
  331.7 184.9 %all-reduce.13.cloned.1.call-start = ((), (), s32[]{:S(2)}) async-start(), calls=%async_computation.3 | async-start | bytes 1048576 | tf_op jit(solution)/shard_map/psum | solution.py:69
  424.9 256.6 %all-reduce.15.cloned.1.call-start = ((), (), s32[]{:S(2)}) async-start(), calls=%async_computation.4 | async-start | bytes 1048576 | tf_op jit(solution)/shard_map/pmax | solution.py:67
  589.6 0.8 copy-start.2
  590.5 185.3 %all-reduce.17.cloned.1.call-start = ((), (), s32[]{:S(2)}) async-start(), calls=%async_computation.5 | async-start | bytes 1048576 | tf_op jit(solution)/shard_map/psum | solution.py:69
Sparse Core Ops, SparseCore 0:
  70.6 93.0 all-reduce.6
  167.5 90.5 all-reduce.8
  331.9 90.8 all-reduce.10
  426.1 90.5 all-reduce.12
  590.6 90.8 all-reduce.14
  685.1 90.5 all-reduce.16
where the time goes:
time: 826 us; the launch traced here: 823 us
  waiting for transfers between devices  550 us (67%)
  local copies, waits for them, and re-layouts  115 us (14%)
  other arithmetic  81.1 us (10%)
  matrix products  35.6 us (4%)
  loops' own time  26.3 us (3%)
  between operations  14.4 us (2%)
    pmax x3, waiting for transfers between devices, local(): global_max = lax.pmax(running_max, 'row')  275 us
    psum x3, waiting for transfers between devices, local(): summed = lax.psum(scaled, 'row')  274 us
    gather x24, local copies, waits for them, and re-layouts, block_scores(): picked = target_blocks[columns].reshape(slots * BLOCK, width)  56.8 us
    dot_general x24, matrix products, block_scores(): lax.dot_general(source_blocks[which], picked, (((1,), (1,)), ((), ())), p...  35.6 us
    unnamed x20, local copies, waits for them, and re-layouts  33.7 us
    reduce_sum x12, other arithmetic, row_step(): summed_row = jnp.sum(jnp.exp(scores - top[:, None, None]), axis=(1, 2))  25.8 us
    another operation x3, loops' own time, local(): source_pot = lax.map(row_step, jnp.arange(own_blocks, dtype=jnp.int32))  25.4 us
    reduce_sum x12, other arithmetic, column_step(): block_sum = jnp.sum(jnp.exp(scores - block_max[None]), axis=0)  19.7 us
  transfers between devices with their start and end apart: 6, of which 6 were waited for; matrix products, arithmetic and copies ran while one was open for 0% of the time, Pallas kernels for 0%

commit v1 on v0

v1 whole, which is shorter than its diff:
```python
import functools

import jax
import jax.numpy as jnp
from jax import lax
from jax.experimental import pallas as pl
from jax.experimental.pallas import tpu as pltpu
from jax.sharding import PartitionSpec as P

BLOCK = 256
ITERS = 3
FLOOR = -1e30
GROUP = 2
ROWS = 32
VMEM_BYTES = 52 * 1024 * 1024


def scores_of(source_ref, gathered, which, slot, slots):
    source = source_ref[pl.ds(pl.multiple_of(which * BLOCK, BLOCK), BLOCK), :]
    return jnp.dot(source, gathered[which * slots + slot], preferred_element_type=jnp.float32)


def fetch(columns_ref, targets_ref, gathered, sems, which, slot, slots):
    column = columns_ref[which, slot]
    return pltpu.make_async_copy(
        targets_ref.at[:, pl.ds(pl.multiple_of(column * BLOCK, BLOCK), BLOCK)],
        gathered.at[which * slots + slot],
        sems.at[which * slots + slot],
    )


def rounded(count):
    return (count + GROUP - 1) // GROUP


def start_all(columns_ref, counts_ref, targets_ref, gathered, sems):
    own, slots = columns_ref.shape

    def one_source(which, _):
        def one(slot, _):
            fetch(columns_ref, targets_ref, gathered, sems, which, slot, slots).start()
            return 0

        return lax.fori_loop(0, rounded(counts_ref[which]) * GROUP, one, 0)

    lax.fori_loop(0, own, one_source, 0)


def row_of(columns_ref, counts_ref, which, slot, target_count):
    return jnp.where(slot < counts_ref[which], columns_ref[which, slot], target_count)


def clear(ref, target_count, value):
    own = ref.shape[0]

    def one(i, _):
        rows = pl.ds(pl.multiple_of(i * ROWS, ROWS), ROWS)
        for p in range(own):
            ref[p, rows, :] = jnp.full((ROWS, BLOCK), value, jnp.float32)
        return 0

    lax.fori_loop(0, target_count // ROWS, one, 0)


def first_columns(
    columns_ref, counts_ref, source_ref, targets_ref, out_ref, gathered, tops, sums, sems
):
    own, slots = columns_ref.shape
    target_count = out_ref.shape[0]
    start_all(columns_ref, counts_ref, targets_ref, gathered, sems)
    clear(tops, target_count, FLOOR)
    clear(sums, target_count, 0.0)

    def one_source(which, _):
        def group(i, _):
            for k in range(GROUP):
                slot = i * GROUP + k
                fetch(columns_ref, targets_ref, gathered, sems, which, slot, slots).wait()
            for k in range(GROUP):
                slot = i * GROUP + k
                scores = scores_of(source_ref, gathered, which, slot, slots)
                top = jnp.max(scores, axis=0, keepdims=True)
                total = jnp.sum(jnp.exp(scores - top), axis=0, keepdims=True)
                row = row_of(columns_ref, counts_ref, which, slot, target_count)
                tops[which, pl.ds(row, 1), :] = top
                sums[which, pl.ds(row, 1), :] = total
            return 0

        return lax.fori_loop(0, rounded(counts_ref[which]), group, 0)

    lax.fori_loop(0, own, one_source, 0)

    def combine(i, _):
        rows = pl.ds(pl.multiple_of(i * ROWS, ROWS), ROWS)
        top = tops[0, rows, :]
        for p in range(1, own):
            top = jnp.maximum(top, tops[p, rows, :])
        total = jnp.zeros_like(top)
        for p in range(own):
            total = total + sums[p, rows, :] * jnp.exp(tops[p, rows, :] - top)
        used = total > 0.0
        out_ref[rows, :] = jnp.where(used, top + jnp.log(jnp.where(used, total, 1.0)), FLOOR)
        return 0

    lax.fori_loop(0, target_count // ROWS, combine, 0)


def halves(x):
    return x[:, : BLOCK // 2], x[:, BLOCK // 2 :]


def rows_kernel(
    first,
    columns_out,
    columns_ref,
    counts_ref,
    source_ref,
    weights_ref,
    old_ref,
    pot_ref,
    targets_ref,
    new_ref,
    *rest,
):
    if columns_out:
        out_ref, gathered, held, partial, sems, dense = rest
    else:
        gathered, held, partial, sems = rest
    own, slots = columns_ref.shape
    target_count = pot_ref.shape[0]
    start_all(columns_ref, counts_ref, targets_ref, gathered, sems)
    if columns_out:
        clear(dense, target_count, 0.0)

    def one_source(which, _):
        own_rows = pl.ds(pl.multiple_of(which * BLOCK, BLOCK), BLOCK)
        groups = rounded(counts_ref[which])

        def wait(i):
            for k in range(GROUP):
                slot = i * GROUP + k
                fetch(columns_ref, targets_ref, gathered, sems, which, slot, slots).wait()

        def shifted(slot):
            scores = scores_of(source_ref, gathered, which, slot, slots)
            column = columns_ref[which, slot]
            pot = pot_ref[pl.ds(column, 1), :] + jnp.where(slot < counts_ref[which], 0.0, FLOOR)
            return scores + pot

        if first:
            partial[...] = jnp.full(partial.shape, FLOOR, jnp.float32)

            def top_group(i, _):
                wait(i)
                best = partial[...]
                for k in range(GROUP):
                    low, high = halves(shifted(i * GROUP + k))
                    best = jnp.maximum(best, jnp.maximum(low, high))
                partial[...] = best
                return 0

            lax.fori_loop(0, groups, top_group, 0)
            offset = -jnp.max(partial[...], axis=1, keepdims=True)
        else:
            offset = old_ref[own_rows, :]

        partial[...] = jnp.zeros(partial.shape, jnp.float32)

        def sum_group(i, _):
            if not first:
                wait(i)
            total = partial[...]
            for k in range(GROUP):
                slot = i * GROUP + k
                terms = jnp.exp(shifted(slot) + offset)
                if columns_out:
                    held[slot] = terms
                low, high = halves(terms)
                total = total + (low + high)
            partial[...] = total
            return 0

        lax.fori_loop(0, groups, sum_group, 0)
        total = jnp.sum(partial[...], axis=1, keepdims=True)
        weights = weights_ref[own_rows, :]
        new_ref[own_rows, :] = weights + offset - jnp.log(total)
        if columns_out:
            factor = jnp.exp(weights) / total

            def column_group(i, _):
                for k in range(GROUP):
                    slot = i * GROUP + k
                    row = row_of(columns_ref, counts_ref, which, slot, target_count)
                    dense[which, pl.ds(row, 1), :] = jnp.sum(
                        held[slot] * factor, axis=0, keepdims=True
                    )
                return 0

            lax.fori_loop(0, groups, column_group, 0)
        return 0

    lax.fori_loop(0, own, one_source, 0)

    if columns_out:

        def combine(i, _):
            rows = pl.ds(pl.multiple_of(i * ROWS, ROWS), ROWS)
            total = dense[0, rows, :]
            for p in range(1, own):
                total = total + dense[p, rows, :]
            out_ref[rows, :] = total
            return 0

        lax.fori_loop(0, target_count // ROWS, combine, 0)


def stages_of(devices):
    radices = []
    rest = devices
    if rest % 2 == 0:
        radices.append(2)
        rest //= 2
    while rest > 1:
        if rest % 4 == 0 and (rest & (rest - 1)) == 0 and rest.bit_length() % 2 == 1:
            radix = 4
        elif rest % 2 == 0:
            radix = 2
        else:
            radix = rest
        radices.append(radix)
        rest //= radix
    stages = []
    stride = 1
    for radix in radices:
        stages.append((radix, stride))
        stride *= radix
    return stages


def reduce_kernel(
    first,
    stages,
    term_ref,
    weights_ref,
    old_ref,
    out_ref,
    total,
    landed,
    weights_own,
    old_own,
    send_sems,
    recv_sems,
    local_sems,
):
    me = lax.axis_index("row")
    barrier = pltpu.get_barrier_semaphore()
    greeted = 0
    for radix, stride in stages:
        digit = lax.rem(me // stride, radix)
        for k in range(1, radix):
            peer = me + (lax.rem(digit + k, radix) - digit) * stride
            pl.semaphore_signal(
                barrier, inc=1, device_id={"row": peer}, device_id_type=pl.DeviceIdType.MESH
            )
            greeted += 1
    length = term_ref.shape[0]
    base = 0
    bases = []
    for radix, stride in stages:
        bases.append(base)
        length //= radix
        base = base + lax.rem(me // stride, radix) * length
    own = pl.ds(pl.multiple_of(base, 8), length)
    local = [pltpu.make_async_copy(weights_ref.at[own], weights_own, local_sems.at[0])]
    if not first:
        local.append(pltpu.make_async_copy(old_ref.at[own], old_own, local_sems.at[1]))
    for copy in local:
        copy.start()
    pl.semaphore_wait(barrier, greeted)

    sent = []
    index = 0
    offset = 0
    piece = term_ref.shape[0]
    current = term_ref
    for number, (radix, stride) in enumerate(stages):
        digit = lax.rem(me // stride, radix)
        piece //= radix
        copies = []
        for k in range(1, radix):
            other = lax.rem(digit + k, radix)
            peer = me + (other - digit) * stride
            start = pl.multiple_of(bases[number] + other * piece, 8)
            copy = pltpu.make_async_remote_copy(
                src_ref=current.at[pl.ds(start, piece)],
                dst_ref=landed.at[pl.ds(offset + (k - 1) * piece, piece)],
                send_sem=send_sems.at[index],
                recv_sem=recv_sems.at[index],
                device_id={"row": peer},
                device_id_type=pl.DeviceIdType.MESH,
            )
            copy.start()
            copies.append(copy)
            index += 1
        for copy in copies:
            copy.wait_recv()
        sent += copies
        mine = bases[number] + digit * piece

        def fold(i, _, mine=mine, offset=offset, radix=radix, piece=piece, current=current):
            rows = pl.ds(pl.multiple_of(mine + i * ROWS, 8), ROWS)
            parts = [current[rows, :]]
            for k in range(1, radix):
                start = pl.multiple_of(offset + (k - 1) * piece + i * ROWS, 8)
                parts.append(landed[pl.ds(start, ROWS), :])
            if first:
                top = functools.reduce(jnp.maximum, parts)
                value = top + jnp.log(sum(jnp.exp(part - top) for part in parts))
            else:
                value = sum(parts[1:], parts[0])
            total[rows, :] = value
            return 0

        lax.fori_loop(0, piece // ROWS, fold, 0)
        offset += (radix - 1) * piece
        current = total

    for copy in local:
        copy.wait()

    def finish(i, _):
        rows = pl.ds(pl.multiple_of(base + i * ROWS, 8), ROWS)
        near = pl.ds(pl.multiple_of(i * ROWS, 8), ROWS)
        if first:
            out_ref[rows, :] = weights_own[near, :] - total[rows, :]
        else:
            out_ref[rows, :] = weights_own[near, :] + old_own[near, :] - jnp.log(total[rows, :])
        return 0

    lax.fori_loop(0, piece // ROWS, finish, 0)

    start = base
    for number in reversed(range(len(stages))):
        radix, stride = stages[number]
        digit = lax.rem(me // stride, radix)
        rows = pl.ds(pl.multiple_of(start, 8), piece)
        copies = []
        for k in range(1, radix):
            peer = me + (lax.rem(digit + k, radix) - digit) * stride
            copy = pltpu.make_async_remote_copy(
                src_ref=out_ref.at[rows],
                dst_ref=out_ref.at[rows],
                send_sem=send_sems.at[index],
                recv_sem=recv_sems.at[index],
                device_id={"row": peer},
                device_id_type=pl.DeviceIdType.MESH,
            )
            copy.start()
            copies.append(copy)
            index += 1
        for copy in copies:
            copy.wait_recv()
        sent += copies
        start = bases[number]
        piece *= radix
    for copy in sent:
        copy.wait_send()


def local(
    source_features, target_features, source_weights, target_weights, block_columns, block_counts
):
    own, slots = block_columns.shape
    target_count = target_features.shape[0] // BLOCK
    width = target_features.shape[1]
    cells = source_features.shape[0]
    devices = lax.axis_size("row")
    stages = stages_of(devices)
    share = target_count // devices
    targets = target_features.T
    weights_tgt = target_weights.reshape(target_count, BLOCK)
    weights_src = source_weights.reshape(cells, 1)

    in_smem = pl.BlockSpec(memory_space=pltpu.SMEM)
    in_vmem = pl.BlockSpec(memory_space=pltpu.VMEM)
    anywhere = pl.BlockSpec(memory_space=pl.ANY)
    params = pltpu.CompilerParams(vmem_limit_bytes=VMEM_BYTES)
    gathered = pltpu.VMEM((own * slots, width, BLOCK), source_features.dtype)
    fetches = pltpu.SemaphoreType.DMA((own * slots,))
    dense = pltpu.VMEM((own, target_count + 8, BLOCK), jnp.float32)
    whole = jax.ShapeDtypeStruct((target_count, BLOCK), jnp.float32)
    per_source = jax.ShapeDtypeStruct((cells, 1), jnp.float32)

    first_term = pl.pallas_call(
        first_columns,
        out_shape=whole,
        in_specs=[in_smem, in_smem, in_vmem, anywhere],
        out_specs=in_vmem,
        scratch_shapes=[gathered, dense, dense, fetches],
        compiler_params=params,
        name="first_columns",
    )

    def rows(first, columns_out):
        scratch = [
            gathered,
            pltpu.VMEM((slots, BLOCK, BLOCK), jnp.float32),
            pltpu.VMEM((BLOCK, BLOCK // 2), jnp.float32),
            fetches,
        ]
        return pl.pallas_call(
            functools.partial(rows_kernel, first, columns_out),
            out_shape=(per_source, whole) if columns_out else per_source,
            in_specs=[in_smem, in_smem, in_vmem, in_vmem, in_vmem, in_vmem, anywhere],
            out_specs=(in_vmem, in_vmem) if columns_out else in_vmem,
            scratch_shapes=scratch + ([dense] if columns_out else []),
            compiler_params=params,
            name="rows",
        )

    messages = 2 * sum(radix - 1 for radix, _ in stages)
    landing = 0
    piece = target_count
    for radix, _ in stages:
        piece //= radix
        landing += (radix - 1) * piece

    def reduce_call(first):
        return pl.pallas_call(
            functools.partial(reduce_kernel, first, stages),
            out_shape=whole,
            in_specs=[in_vmem, anywhere, anywhere],
            out_specs=in_vmem,
            scratch_shapes=[
                pltpu.VMEM((target_count, BLOCK), jnp.float32),
                pltpu.VMEM((landing, BLOCK), jnp.float32),
                pltpu.VMEM((share, BLOCK), jnp.float32),
                pltpu.VMEM((share, BLOCK), jnp.float32),
                pltpu.SemaphoreType.DMA((messages,)),
                pltpu.SemaphoreType.DMA((messages,)),
                pltpu.SemaphoreType.DMA((2,)),
            ],
            compiler_params=pltpu.CompilerParams(
                vmem_limit_bytes=VMEM_BYTES,
                collective_id=0 if first else 1,
                has_side_effects=True,
            ),
            name="reduce",
        )

    term = first_term(block_columns, block_counts, source_features, targets)
    target_pot = reduce_call(True)(term, weights_tgt, weights_tgt)
    source_pot = weights_src
    for sweep in range(ITERS):
        last = sweep == ITERS - 1
        result = rows(sweep == 0, not last)(
            block_columns, block_counts, source_features, weights_src, source_pot, target_pot, targets
        )
        if last:
            source_pot = result
        else:
            source_pot, term = result
            target_pot = reduce_call(False)(term, weights_tgt, target_pot)
    position = lax.axis_index("row")
    own_pot = lax.dynamic_slice_in_dim(target_pot, position * share, share, 0)
    return (source_pot.reshape(-1), own_pot.reshape(-1))


def solution(mesh):
    return jax.shard_map(
        local,
        mesh=mesh,
        in_specs=(
            P(("groups", "row"), None),
            P("groups", None),
            P(("groups", "row")),
            P("groups"),
            P(("groups", "row"), None),
            P(("groups", "row")),
        ),
        out_specs=(P(("groups", "row")), P(("groups", "row"))),
        check_vma=False,
    )
```

time: 826 us -> 173 us (0.21)
  waiting for transfers between devices: 550 us -> 0 us
  Pallas kernels: 0 us -> 162 us
  local copies, waits for them, and re-layouts: 115 us -> 7.33 us
  other arithmetic: 81.1 us -> 0.8 us
  matrix products: 35.6 us -> 0 us
  loops' own time: 26.3 us -> 0 us
  between operations: 14.4 us -> 0.8 us
    pmax x3 -> x0, waiting for transfers between devices: 275 us -> none  [local(): global_max = lax.pmax(running_max, 'row')]
    psum x3 -> x0, waiting for transfers between devices: 274 us -> none  [local(): summed = lax.psum(scaled, 'row')]
    pallas_call x0 -> x7, Pallas kernels: none -> 162 us  [the longest x3 68.4 us: local(): rows(sweep == 0, not last)]
    gather x48 -> x0, local copies, waits for them, and re-layouts: 71.3 us -> none  [the longest x24 56.8 us: block_scores(): picked = target_blocks[columns].reshape(slots * BLOCK, width)]
    reduce_sum x24 -> x0, other arithmetic: 45.5 us -> none  [the longest x12 25.8 us: row_step(): summed_row = jnp.sum(jnp.exp(scores - top[:, None, None]), axis=(1, 2))]
    dot_general x24 -> x0, matrix products: 35.6 us -> none  [block_scores(): lax.dot_general(source_blocks[which], picked, (((1,), (1,)), ((), ())), p...]
    unnamed x20 -> x23, local copies, waits for them, and re-layouts: 33.7 us -> 6.96 us
    another operation x6 -> x0, loops' own time: 26.3 us -> none  [the longest x3 25.4 us: local(): source_pot = lax.map(row_step, jnp.arange(own_blocks, dtype=jnp.int32))]
  transfers between devices with their start and end apart: 6 -> 0, of which waited for: 6 -> 0; matrix products, arithmetic and copies ran while one was open for 0% -> 0% of each run, Pallas kernels for 0% -> 0%
where the time goes in v1:
time: 173 us; the launch traced here: 171 us
  Pallas kernels  162 us (94%)
  local copies, waits for them, and re-layouts  7.33 us (4%)
    pallas_call x3, Pallas kernels, local(): rows(sweep == 0, not last)  68.4 us
    pallas_call x2, Pallas kernels, local(): target_pot = reduce_call(False)(term, weights_tgt, target_pot)  49.2 us
    pallas_call x1, Pallas kernels, local(): target_pot = reduce_call(True)(term, weights_tgt, weights_tgt)  25.3 us
    pallas_call x1, Pallas kernels, local(): term = first_term(block_columns, block_counts, source_features, targets)  19.2 us
    unnamed x23, local copies, waits for them, and re-layouts  6.96 us

profile of v1, /device:TPU:0, one launch (start us, length us, event | category | flops | bytes accessed | tf_op | source)
XLA Modules:
  0.0 171.0 jit_solution(17115305345066065182)
XLA Ops:
  0.6 0.0 copy-start.5
  0.6 0.0 copy-start.7
  0.7 0.0 copy-start.9
  0.7 1.1 copy.18.source_ref
  1.8 0.0 copy-start.4
  1.8 0.7 copy-done.4
  2.4 0.0 copy-start.6
  2.4 0.7 copy-done.6
  3.1 0.0 copy-start.8
  3.1 19.2 %first_columns.1.term_ref = f32[512,256]{1,0:T(8,128)S(1)} custom-call(s32[4,32]{1,0:T(4,128)S(1)} %copy-done.4, s32[4]{0:T(128)S(1)} %copy-done.6, bf16[1024,64]{1,0:T(8,128)(2,1)S(1)} %copy.18.source_ref, bf16[64,131072]{1,0:T(8,128)(2,1)} %bitcast.5), custom_call_target="tpu_custom_call" | custom-call | tf_op jit(solution)/shard_map/first_columns/pallas_call | solution.py:451
  22.3 0.0 copy-done.8
  22.3 0.1 reshape.17.weights_ref.old_ref
  22.5 25.3 %reduce.4.pot_ref.old_ref = f32[512,256]{1,0:T(8,128)S(1)} custom-call(f32[512,256]{1,0:T(8,128)S(1)} %first_columns.1.term_ref, f32[512,256]{1,0:T(8,128)S(1)} %reshape.17.weights_ref.old_ref, f32[512,256]{1,0:T(8,128)S(1)} %reshape.17.weights_ref.old_ref), custom_call_target="tpu_custom_call" | custom-call | tf_op jit(solution)/shard_map/reduce/pallas_call | solution.py:452
  47.8 0.0 copy-start.1
  47.8 0.8 copy-done.1
  48.6 0.0 copy-done.9
  48.6 0.2 copy.19.weights_ref.old_ref
  48.8 0.0 copy-done.5
  48.8 0.0 copy-done.7
  48.8 31.8 %rows.3 = (f32[1024,1]{1,0:T(8,128)S(1)}, f32[512,256]{1,0:T(8,128)S(1)}) custom-call(s32[4,32]{1,0:T(4,128)S(1)} %copy-done.5, s32[4]{0:T(128)S(1)} %copy-done.7, bf16[1024,64]{1,0:T(8,128)(2,1)S(1)} %copy.18.source_ref, f32[1024,1]{1,0:T(8,128)S(1)} %copy.19.weights_ref.old_ref, f32[1024,1]{1,0:T(8,128)S(1)} %copy.19.weights_ref.old_ref, ...), custom_call_target="tpu_custom_call" | custom-call | tf_op jit(solution)/shard_map/rows/pallas_call | solution.py:456
  80.6 0.0 copy-start.3
  80.7 0.8 copy-done.3
  81.4 25.0 %reduce.5.pot_ref.old_ref = f32[512,256]{1,0:T(8,128)S(1)} custom-call(f32[512,256]{1,0:T(8,128)S(1)} %get-tuple-element.7.term_ref, f32[512,256]{1,0:T(8,128)S(1)} %reshape.17.weights_ref.old_ref, f32[512,256]{1,0:T(8,128)} %copy-done.1), custom_call_target="tpu_custom_call" | custom-call | tf_op jit(solution)/shard_map/reduce/pallas_call | solution.py:463
  106.4 0.0 copy-start
  106.4 0.8 copy-done
  107.2 21.4 %rows.4 = (f32[1024,1]{1,0:T(8,128)S(1)}, f32[512,256]{1,0:T(8,128)S(1)}) custom-call(s32[4,32]{1,0:T(4,128)S(1)} %copy-done.5, s32[4]{0:T(128)S(1)} %copy-done.7, bf16[1024,64]{1,0:T(8,128)(2,1)S(1)} %copy.18.source_ref, f32[1024,1]{1,0:T(8,128)S(1)} %copy.19.weights_ref.old_ref, f32[1024,1]{1,0:T(8,128)} %copy-done.3, f32[512,256]{1,0:T(8,128)} %copy-done, ...), custom_call_target="tpu_custom_call" | custom-call | tf_op jit(solution)/shard_map/rows/pallas_call | solution.py:456
  128.6 24.2 %reduce.6.pot_ref = f32[512,256]{1,0:T(8,128)S(1)} custom-call(f32[512,256]{1,0:T(8,128)S(1)} %get-tuple-element.9.term_ref, f32[512,256]{1,0:T(8,128)S(1)} %reshape.17.weights_ref.old_ref, f32[512,256]{1,0:T(8,128)} %copy-done), custom_call_target="tpu_custom_call" | custom-call | tf_op jit(solution)/shard_map/reduce/pallas_call | solution.py:463
  152.8 0.0 copy-start.2
  152.8 0.8 copy-done.2
  153.6 15.2 %rows.5 = f32[1024,1]{1,0:T(8,128)S(1)} custom-call(s32[4,32]{1,0:T(4,128)S(1)} %copy-done.5, s32[4]{0:T(128)S(1)} %copy-done.7, bf16[1024,64]{1,0:T(8,128)(2,1)S(1)} %copy.18.source_ref, f32[1024,1]{1,0:T(8,128)S(1)} %copy.19.weights_ref.old_ref, f32[1024,1]{1,0:T(8,128)S(1)} %get-tuple-element.8.old_ref, f32[512,256]{1,0:T(8,128)} %copy-done.2, ...), custom_call_target="tpu_custom_call" | custom-call | tf_op jit(solution)/shard_map/rows/pallas_call | solution.py:456
  168.8 0.8 reduce.3
  169.7 0.8 dynamic-slice_bitcast_fusion
  170.4 0.6 copy.20
Async XLA Ops:
  0.6 48.2 %copy-start.5 = (s32[4,32]{1,0:T(4,128)S(1)}, s32[4,32]{1,0:T(4,128)}, u32[]{:S(2)}) copy-start(s32[4,32]{1,0:T(4,128)} %columns_ref.7) | copy-start | bytes 1540
  0.6 48.2 %copy-start.7 = (s32[4]{0:T(128)S(1)}, s32[4]{0:T(128)}, u32[]{:S(2)}) copy-start(s32[4]{0:T(128)} %counts_ref.7) | copy-start | bytes 52
  0.7 47.9 %copy-start.9 = (f32[1024]{0:T(1024)S(1)}, f32[1024]{0:T(1024)}, u32[]{:S(2)}) copy-start(f32[1024]{0:T(1024)} %param.8) | copy-start | bytes 12292
  1.8 0.7 copy-start.4
  2.4 0.7 copy-start.6
  3.1 19.2 %copy-start.8 = (f32[131072]{0:T(1024)S(1)}, f32[131072]{0:T(1024)}, u32[]{:S(2)}) copy-start(f32[131072]{0:T(1024)} %param.9) | copy-start | bytes 1572868
  47.8 0.8 copy-start.1
  80.6 0.8 copy-start.3
  106.4 0.8 copy-start
  152.8 0.8 copy-start.2

commit v2 on v1

v2 whole, which is shorter than its diff:
```python
import functools

import jax
import jax.numpy as jnp
from jax import lax
from jax.experimental import pallas as pl
from jax.experimental.pallas import tpu as pltpu
from jax.sharding import PartitionSpec as P

BLOCK = 256
ITERS = 3
FLOOR = -1e30
GROUP = 16
ROWS = 32
AHEAD = 2
CHUNKS = 2
EXTRA = 16
HALVES = (pl.ds(0, BLOCK // 2), pl.ds(BLOCK // 2, BLOCK // 2))
VMEM_BYTES = 50 * 1024 * 1024


def scores_of(source_ref, gathered, which, slot, slots, lanes):
    width = gathered.shape[1]
    source = source_ref[pl.ds(pl.multiple_of(which * BLOCK, BLOCK), BLOCK), pl.ds(0, width)]
    targets = gathered[which * slots + slot, :, lanes]
    return jnp.dot(source, targets, preferred_element_type=jnp.float32)


def pieces(x):
    high = x.astype(jnp.bfloat16).astype(jnp.float32)
    rest = x - high
    middle = rest.astype(jnp.bfloat16).astype(jnp.float32)
    return high, middle, rest - middle


def with_pieces(x, index, at, base):
    for k, piece in enumerate(pieces(x)):
        base = jnp.where(index == at + k, piece, base)
    return base


def fetch(columns_ref, targets_ref, gathered, sems, index):
    slots = columns_ref.shape[1]
    column = columns_ref[index // slots, lax.rem(index, slots)]
    return pltpu.make_async_copy(
        targets_ref.at[:, pl.ds(pl.multiple_of(column * BLOCK, BLOCK), BLOCK)],
        gathered.at[index],
        sems.at[index],
    )


def row_of(columns_ref, counts_ref, which, slot, target_count):
    return jnp.where(slot < counts_ref[which], columns_ref[which, slot], target_count)


def clear(ref, target_count, value):
    own = ref.shape[0]

    def one(i, _):
        rows = pl.ds(pl.multiple_of(i * ROWS, ROWS), ROWS)
        for p in range(own):
            ref[p, rows, :] = jnp.full((ROWS, BLOCK), value, jnp.float32)
        return 0

    lax.fori_loop(0, target_count // ROWS, one, 0)


def first_columns(
    columns_ref, counts_ref, source_ref, targets_ref, out_ref, gathered, tops, sums, sems
):
    own, slots = columns_ref.shape
    target_count = out_ref.shape[0]
    groups = own * slots // GROUP

    def start(group):
        for k in range(GROUP):
            fetch(columns_ref, targets_ref, gathered, sems, group * GROUP + k).start()

    for group in range(min(AHEAD, groups)):
        start(group)
    clear(tops, target_count, FLOOR)
    clear(sums, target_count, 0.0)

    def work(group):
        for k in range(GROUP):
            fetch(columns_ref, targets_ref, gathered, sems, group * GROUP + k).wait()
        which = group * GROUP // slots
        for k in range(GROUP):
            slot = lax.rem(group * GROUP, slots) + k
            row = row_of(columns_ref, counts_ref, which, slot, target_count)
            top_parts = []
            sum_parts = []
            for lanes in HALVES:
                scores = scores_of(source_ref, gathered, which, slot, slots, lanes)
                top = jnp.max(scores, axis=0, keepdims=True)
                top_parts.append(top)
                sum_parts.append(jnp.sum(jnp.exp(scores - top), axis=0, keepdims=True))
            tops[which, pl.ds(row, 1), :] = jnp.concatenate(top_parts, axis=1)
            sums[which, pl.ds(row, 1), :] = jnp.concatenate(sum_parts, axis=1)

    def ahead(group, _):
        start(group + AHEAD)
        work(group)
        return 0

    def rest(group, _):
        work(group)
        return 0

    full = max(groups - AHEAD, 0)
    lax.fori_loop(0, full, ahead, 0)
    lax.fori_loop(full, groups, rest, 0)

    def combine(i, _):
        rows = pl.ds(pl.multiple_of(i * ROWS, ROWS), ROWS)
        top = tops[0, rows, :]
        for p in range(1, own):
            top = jnp.maximum(top, tops[p, rows, :])
        total = jnp.zeros_like(top)
        for p in range(own):
            total = total + sums[p, rows, :] * jnp.exp(tops[p, rows, :] - top)
        used = total > 0.0
        out_ref[rows, :] = jnp.where(used, top + jnp.log(jnp.where(used, total, 1.0)), FLOOR)
        return 0

    lax.fori_loop(0, target_count // ROWS, combine, 0)


def halves(x):
    return x[:, : BLOCK // 2], x[:, BLOCK // 2 :]


def rows_kernel(
    first,
    columns_out,
    columns_ref,
    counts_ref,
    source_ref,
    weights_ref,
    old_ref,
    pot_ref,
    gathered,
    new_ref,
    *rest,
):
    if columns_out:
        out_ref, held, partial, source, dense = rest
    else:
        own_ref, partial, source = rest
    own, slots = columns_ref.shape
    target_count = pot_ref.shape[0]
    if columns_out:
        clear(dense, target_count, 0.0)
    else:
        share = own_ref.shape[0]
        mine = pl.multiple_of(lax.axis_index("row") * share, 8)
        own_ref[...] = pot_ref[pl.ds(mine, share), :]
    width = gathered.shape[1]
    extra_row = lax.broadcasted_iota(jnp.int32, (EXTRA, BLOCK), 0)
    ones = jnp.where(extra_row < 3, 1.0, 0.0)
    lane = lax.broadcasted_iota(jnp.int32, (BLOCK, width + EXTRA), 1)

    def one_source(which, _):
        own_rows = pl.ds(pl.multiple_of(which * BLOCK, BLOCK), BLOCK)
        groups = slots // GROUP

        def set_source(offset):
            base = source_ref[own_rows, :].astype(jnp.float32)
            source[...] = with_pieces(offset, lane, width, base).astype(source.dtype)

        def shifted(slot):
            column = columns_ref[which, slot]
            pot = pot_ref[pl.ds(column, 1), :] + jnp.where(slot < counts_ref[which], 0.0, FLOOR)
            extra = with_pieces(pot, extra_row, 3, ones).astype(source.dtype)
            targets = jnp.concatenate([gathered[which * slots + slot], extra], axis=0)
            return jnp.dot(source[...], targets, preferred_element_type=jnp.float32)

        if first:
            set_source(jnp.zeros((BLOCK, 1), jnp.float32))
            partial[...] = jnp.full(partial.shape, FLOOR, jnp.float32)

            def top_group(i, _):
                best = partial[...]
                for k in range(GROUP):
                    low, high = halves(shifted(i * GROUP + k))
                    best = jnp.maximum(best, jnp.maximum(low, high))
                partial[...] = best
                return 0

            lax.fori_loop(0, groups, top_group, 0)
            offset = -jnp.max(partial[...], axis=1, keepdims=True)
        else:
            offset = old_ref[own_rows, :]

        set_source(offset)
        partial[...] = jnp.zeros(partial.shape, jnp.float32)

        def sum_group(i, _):
            total = partial[...]
            for k in range(GROUP):
                slot = i * GROUP + k
                terms = jnp.exp(shifted(slot))
                if columns_out:
                    held[slot] = terms
                low, high = halves(terms)
                total = total + (low + high)
            partial[...] = total
            return 0

        lax.fori_loop(0, groups, sum_group, 0)
        total = jnp.sum(partial[...], axis=1, keepdims=True)
        weights = weights_ref[own_rows, :]
        new_ref[own_rows, :] = weights + offset - jnp.log(total)
        if columns_out:
            partial[...] = jnp.broadcast_to(jnp.exp(weights) / total, partial.shape)

            def column_group(i, _):
                factor = partial[...]
                for k in range(GROUP):
                    slot = i * GROUP + k
                    row = row_of(columns_ref, counts_ref, which, slot, target_count)
                    parts = [
                        jnp.sum(held[slot, :, lanes] * factor, axis=0, keepdims=True)
                        for lanes in HALVES
                    ]
                    dense[which, pl.ds(row, 1), :] = jnp.concatenate(parts, axis=1)
                return 0

            lax.fori_loop(0, groups, column_group, 0)
        return 0

    lax.fori_loop(0, own, one_source, 0)

    if columns_out:

        def combine(i, _):
            rows = pl.ds(pl.multiple_of(i * ROWS, ROWS), ROWS)
            total = dense[0, rows, :]
            for p in range(1, own):
                total = total + dense[p, rows, :]
            out_ref[rows, :] = total
            return 0

        lax.fori_loop(0, target_count // ROWS, combine, 0)


def stages_of(devices):
    radices = []
    rest = devices
    if rest % 2 == 0:
        radices.append(2)
        rest //= 2
    while rest > 1:
        if rest % 4 == 0 and (rest & (rest - 1)) == 0 and rest.bit_length() % 2 == 1:
            radix = 4
        elif rest % 2 == 0:
            radix = 2
        else:
            radix = rest
        radices.append(radix)
        rest //= radix
    stages = []
    stride = 1
    for radix in radices:
        stages.append((radix, stride))
        stride *= radix
    return stages


def reduce_kernel(
    first,
    stages,
    term_ref,
    weights_ref,
    old_ref,
    out_ref,
    total,
    landed,
    weights_own,
    old_own,
    send_sems,
    recv_sems,
    local_sems,
):
    me = lax.axis_index("row")
    barrier = pltpu.get_barrier_semaphore()
    greeted = 0
    for radix, stride in stages:
        digit = lax.rem(me // stride, radix)
        for k in range(1, radix):
            peer = me + (lax.rem(digit + k, radix) - digit) * stride
            pl.semaphore_signal(
                barrier, inc=1, device_id={"row": peer}, device_id_type=pl.DeviceIdType.MESH
            )
            greeted += 1
    chunk = term_ref.shape[0] // CHUNKS
    share = chunk
    for radix, _ in stages:
        share //= radix
    orders = []
    bases = []
    for c in range(CHUNKS):
        rest = stages[1:]
        turn = c % len(rest) if rest else 0
        orders.append(stages[:1] + rest[turn:] + rest[:turn])
        base = c * chunk
        piece = chunk
        levels = [base]
        for radix, stride in orders[c]:
            piece //= radix
            base = base + lax.rem(me // stride, radix) * piece
            levels.append(base)
        bases.append(levels)
    local = []
    for c in range(CHUNKS):
        rows = pl.ds(pl.multiple_of(bases[c][-1], 8), share)
        near = pl.ds(c * share, share)
        sources = [(weights_ref, weights_own)] if first else [
            (weights_ref, weights_own), (old_ref, old_own)
        ]
        for source, target in sources:
            local.append(
                pltpu.make_async_copy(source.at[rows], target.at[near], local_sems.at[len(local)])
            )
    for copy in local:
        copy.start()
    pl.semaphore_wait(barrier, greeted)

    sent = []

    def send(source, start, target, target_start, size, peer):
        index = len(sent)
        copy = pltpu.make_async_remote_copy(
            src_ref=source.at[pl.ds(pl.multiple_of(start, 8), size)],
            dst_ref=target.at[pl.ds(pl.multiple_of(target_start, 8), size)],
            send_sem=send_sems.at[index],
            recv_sem=recv_sems.at[index],
            device_id={"row": peer},
            device_id_type=pl.DeviceIdType.MESH,
        )
        copy.start()
        sent.append(copy)
        return copy

    flying = [[] for _ in range(CHUNKS)]
    places = [0] * CHUNKS
    sizes = [chunk] * CHUNKS
    offset = 0

    def fold(c, number):
        radix, _ = orders[c][number]
        size = sizes[c]
        step = min(ROWS, size)
        mine = bases[c][number + 1]
        place = places[c]
        current = term_ref if number == 0 else total
        last = number == len(stages) - 1

        def one(i, _):
            rows = pl.ds(pl.multiple_of(mine + i * step, 8), step)
            parts = [current[rows, :]]
            for k in range(1, radix):
                start = pl.multiple_of(place + (k - 1) * size + i * step, 8)
                parts.append(landed[pl.ds(start, step), :])
            if first:
                top = functools.reduce(jnp.maximum, parts)
                value = top + jnp.log(sum(jnp.exp(part - top) for part in parts))
            else:
                value = sum(parts[1:], parts[0])
            if last:
                near = pl.ds(pl.multiple_of(c * share + i * step, 8), step)
                if first:
                    out_ref[rows, :] = weights_own[near, :] - value
                else:
                    out_ref[rows, :] = weights_own[near, :] + old_own[near, :] - jnp.log(value)
            else:
                total[rows, :] = value
            return 0

        lax.fori_loop(0, size // step, one, 0)

    for number in range(len(stages) + 1):
        if number == len(stages):
            for copy in local:
                copy.wait()
        for c in range(CHUNKS):
            for copy in flying[c]:
                copy.wait_recv()
            if number > 0:
                fold(c, number - 1)
            if number == len(stages):
                continue
            radix, stride = orders[c][number]
            digit = lax.rem(me // stride, radix)
            sizes[c] //= radix
            places[c] = offset
            flying[c] = []
            for k in range(1, radix):
                other = lax.rem(digit + k, radix)
                flying[c].append(
                    send(
                        term_ref if number == 0 else total,
                        bases[c][number] + other * sizes[c],
                        landed,
                        offset,
                        sizes[c],
                        me + (other - digit) * stride,
                    )
                )
                offset += sizes[c]

    flying = [[] for _ in range(CHUNKS)]
    for number in reversed(range(len(stages))):
        for c in range(CHUNKS):
            for copy in flying[c]:
                copy.wait_recv()
            radix, stride = orders[c][number]
            digit = lax.rem(me // stride, radix)
            start = bases[c][number + 1]
            flying[c] = []
            for k in range(1, radix):
                other = lax.rem(digit + k, radix)
                flying[c].append(
                    send(out_ref, start, out_ref, start, sizes[c], me + (other - digit) * stride)
                )
            sizes[c] *= radix
    for c in range(CHUNKS):
        for copy in flying[c]:
            copy.wait_recv()
    for copy in sent:
        copy.wait_send()


def local(
    source_features, target_features, source_weights, target_weights, block_columns, block_counts
):
    own, slots = block_columns.shape
    target_count = target_features.shape[0] // BLOCK
    width = target_features.shape[1]
    cells = source_features.shape[0]
    carriers = jnp.broadcast_to(
        jnp.where((jnp.arange(EXTRA) >= 3) & (jnp.arange(EXTRA) < 6), 1.0, 0.0), (cells, EXTRA)
    )
    sources = jnp.concatenate([source_features, carriers.astype(source_features.dtype)], axis=1)
    devices = lax.axis_size("row")
    stages = stages_of(devices)
    share = target_count // devices
    targets = target_features.T
    weights_tgt = target_weights.reshape(target_count, BLOCK)
    weights_src = source_weights.reshape(cells, 1)

    in_smem = pl.BlockSpec(memory_space=pltpu.SMEM)
    in_vmem = pl.BlockSpec(memory_space=pltpu.VMEM)
    anywhere = pl.BlockSpec(memory_space=pl.ANY)
    in_hbm = pl.BlockSpec(memory_space=pltpu.HBM)
    params = pltpu.CompilerParams(vmem_limit_bytes=VMEM_BYTES)
    gathered = jax.ShapeDtypeStruct((own * slots, width, BLOCK), source_features.dtype)
    fetches = pltpu.SemaphoreType.DMA((own * slots,))
    dense = pltpu.VMEM((own, target_count + 8, BLOCK), jnp.float32)
    whole = jax.ShapeDtypeStruct((target_count, BLOCK), jnp.float32)
    part = jax.ShapeDtypeStruct((share, BLOCK), jnp.float32)
    per_source = jax.ShapeDtypeStruct((cells, 1), jnp.float32)

    first_term = pl.pallas_call(
        first_columns,
        out_shape=(whole, gathered),
        in_specs=[in_smem, in_smem, in_vmem, in_hbm],
        out_specs=(in_vmem, in_vmem),
        scratch_shapes=[dense, dense, fetches],
        compiler_params=params,
        name="first_columns",
    )

    def rows(first, columns_out):
        partial = pltpu.VMEM((BLOCK, BLOCK // 2), jnp.float32)
        source = pltpu.VMEM((BLOCK, width + EXTRA), source_features.dtype)
        held = pltpu.VMEM((slots, BLOCK, BLOCK), jnp.float32)
        return pl.pallas_call(
            functools.partial(rows_kernel, first, columns_out),
            out_shape=(per_source, whole if columns_out else part),
            in_specs=[in_smem, in_smem, in_vmem, in_vmem, in_vmem, in_vmem, in_vmem],
            out_specs=(in_vmem, in_vmem),
            scratch_shapes=[held, partial, source, dense] if columns_out else [partial, source],
            compiler_params=params,
            name="rows",
        )

    messages = 2 * CHUNKS * sum(radix - 1 for radix, _ in stages)

    def reduce_call(first):
        return pl.pallas_call(
            functools.partial(reduce_kernel, first, stages),
            out_shape=whole,
            in_specs=[in_vmem, anywhere, anywhere],
            out_specs=in_vmem,
            scratch_shapes=[
                pltpu.VMEM((target_count, BLOCK), jnp.float32),
                pltpu.VMEM((target_count, BLOCK), jnp.float32),
                pltpu.VMEM((share, BLOCK), jnp.float32),
                pltpu.VMEM((share, BLOCK), jnp.float32),
                pltpu.SemaphoreType.DMA((messages,)),
                pltpu.SemaphoreType.DMA((messages,)),
                pltpu.SemaphoreType.DMA((2 * CHUNKS,)),
            ],
            compiler_params=pltpu.CompilerParams(
                vmem_limit_bytes=VMEM_BYTES,
                collective_id=0 if first else 1,
                has_side_effects=True,
            ),
            name="reduce",
        )

    term, picked = first_term(block_columns, block_counts, sources, targets)
    target_pot = reduce_call(True)(term, weights_tgt, weights_tgt)
    source_pot = weights_src
    for sweep in range(ITERS):
        last = sweep == ITERS - 1
        source_pot, term = rows(sweep == 0, not last)(
            block_columns, block_counts, sources, weights_src, source_pot, target_pot, picked
        )
        if not last:
            target_pot = reduce_call(False)(term, weights_tgt, target_pot)
    return (source_pot.reshape(-1), term.reshape(-1))


def solution(mesh):
    return jax.shard_map(
        local,
        mesh=mesh,
        in_specs=(
            P(("groups", "row"), None),
            P("groups", None),
            P(("groups", "row")),
            P("groups"),
            P(("groups", "row"), None),
            P(("groups", "row")),
        ),
        out_specs=(P(("groups", "row")), P(("groups", "row"))),
        check_vma=False,
    )
```

time: 173 us -> 127 us (0.73)
  Pallas kernels: 162 us -> 120 us
  local copies, waits for them, and re-layouts: 7.33 us -> 5.22 us
    pallas_call x3, Pallas kernels: 68.4 us -> 39.4 us  [local(): rows(sweep == 0, not last)]
    pallas_call x2, Pallas kernels: 49.2 us -> 41.7 us  [local(): target_pot = reduce_call(False)(term, weights_tgt, target_pot)]
    unnamed x23 -> x6, local copies, waits for them, and re-layouts: 6.96 us -> 3.03 us
    pallas_call x1, Pallas kernels: 19.2 us -> 15.6 us  [local(): term, picked = first_term(block_columns, block_counts, sources, targets)]
    pallas_call x1, Pallas kernels: 25.3 us -> 22.9 us  [local(): target_pot = reduce_call(True)(term, weights_tgt, weights_tgt)]
where the time goes in v2:
time: 127 us; the launch traced here: 126 us
  Pallas kernels  120 us (94%)
  local copies, waits for them, and re-layouts  5.22 us (4%)
    pallas_call x2, Pallas kernels, local(): target_pot = reduce_call(False)(term, weights_tgt, target_pot)  41.7 us
    pallas_call x3, Pallas kernels, local(): rows(sweep == 0, not last)  39.4 us
    pallas_call x1, Pallas kernels, local(): target_pot = reduce_call(True)(term, weights_tgt, weights_tgt)  22.9 us
    pallas_call x1, Pallas kernels, local(): term, picked = first_term(block_columns, block_counts, sources, targets)  15.6 us
    unnamed x6, local copies, waits for them, and re-layouts  3.03 us

profile of v2, /device:TPU:0, one launch (start us, length us, event | category | flops | bytes accessed | tf_op | source)
XLA Modules:
  0.0 126.4 jit_solution(10204011740181792055)
XLA Ops:
  0.6 0.1 pad.1.clone
  0.7 1.1 copy.9
  1.8 0.1 pad_maximum_fusion.source_ref
  1.9 0.9 copy.13.weights_ref.old_ref
  2.8 1.2 reshape.17.weights_ref.old_ref
  4.0 0.0 copy-start
  4.0 0.7 copy-done
  4.7 0.0 copy-start.1
  4.7 0.7 copy-done.1
  5.3 15.6 %first_columns.1 = (f32[512,256]{1,0:T(8,128)S(1)}, bf16[128,64,256]{2,1,0:T(8,128)(2,1)}) custom-call(s32[4,32]{1,0:T(4,128)S(1)} %copy-done, s32[4]{0:T(128)S(1)} %copy-done.1, bf16[1024,80]{1,0:T(8,128)(2,1)S(1)} %pad_maximum_fusion.source_ref, bf16[64,131072]{1,0:T(8,128)(2,1)} %bitcast.5), custom_call_target="tpu_custom_call" | custom-call | tf_op jit(solution)/shard_map/first_columns/pallas_call | solution.py:513
  21.0 22.9 %reduce.4.pot_ref.old_ref = f32[512,256]{1,0:T(8,128)S(1)} custom-call(f32[512,256]{1,0:T(8,128)S(1)} %get-tuple-element.10.term_ref, f32[512,256]{1,0:T(8,128)S(1)} %reshape.17.weights_ref.old_ref, f32[512,256]{1,0:T(8,128)S(1)} %reshape.17.weights_ref.old_ref), custom_call_target="tpu_custom_call" | custom-call | tf_op jit(solution)/shard_map/reduce/pallas_call | solution.py:514
  43.9 18.1 %rows.3 = (f32[1024,1]{1,0:T(8,128)S(1)}, f32[512,256]{1,0:T(8,128)S(1)}) custom-call(s32[4,32]{1,0:T(4,128)S(1)} %copy-done, s32[4]{0:T(128)S(1)} %copy-done.1, bf16[1024,80]{1,0:T(8,128)(2,1)S(1)} %pad_maximum_fusion.source_ref, f32[1024,1]{1,0:T(8,128)S(1)} %copy.13.weights_ref.old_ref, f32[1024,1]{1,0:T(8,128)S(1)} %copy.13.weights_ref.old_ref, ...), custom_call_target="tpu_custom_call" | custom-call | tf_op jit(solution)/shard_map/rows/pallas_call | solution.py:518
  62.0 20.7 %reduce.5.pot_ref.old_ref = f32[512,256]{1,0:T(8,128)S(1)} custom-call(f32[512,256]{1,0:T(8,128)S(1)} %get-tuple-element.13.term_ref, f32[512,256]{1,0:T(8,128)S(1)} %reshape.17.weights_ref.old_ref, f32[512,256]{1,0:T(8,128)S(1)} %reduce.4.pot_ref.old_ref), custom_call_target="tpu_custom_call" | custom-call | tf_op jit(solution)/shard_map/reduce/pallas_call | solution.py:522
  82.7 12.3 %rows.4 = (f32[1024,1]{1,0:T(8,128)S(1)}, f32[512,256]{1,0:T(8,128)S(1)}) custom-call(s32[4,32]{1,0:T(4,128)S(1)} %copy-done, s32[4]{0:T(128)S(1)} %copy-done.1, bf16[1024,80]{1,0:T(8,128)(2,1)S(1)} %pad_maximum_fusion.source_ref, f32[1024,1]{1,0:T(8,128)S(1)} %copy.13.weights_ref.old_ref, f32[1024,1]{1,0:T(8,128)S(1)} %get-tuple-element.12.old_ref, ...), custom_call_target="tpu_custom_call" | custom-call | tf_op jit(solution)/shard_map/rows/pallas_call | solution.py:518
  95.0 21.1 %reduce.6.pot_ref = f32[512,256]{1,0:T(8,128)S(1)} custom-call(f32[512,256]{1,0:T(8,128)S(1)} %get-tuple-element.15.term_ref, f32[512,256]{1,0:T(8,128)S(1)} %reshape.17.weights_ref.old_ref, f32[512,256]{1,0:T(8,128)S(1)} %reduce.5.pot_ref.old_ref), custom_call_target="tpu_custom_call" | custom-call | tf_op jit(solution)/shard_map/reduce/pallas_call | solution.py:522
  116.1 8.9 %rows.5 = (f32[1024,1]{1,0:T(8,128)S(1)}, f32[32,256]{1,0:T(8,128)S(1)}) custom-call(s32[4,32]{1,0:T(4,128)S(1)} %copy-done, s32[4]{0:T(128)S(1)} %copy-done.1, bf16[1024,80]{1,0:T(8,128)(2,1)S(1)} %pad_maximum_fusion.source_ref, f32[1024,1]{1,0:T(8,128)S(1)} %copy.13.weights_ref.old_ref, f32[1024,1]{1,0:T(8,128)S(1)} %get-tuple-element.14.old_ref, ...), custom_call_target="tpu_custom_call" | custom-call | tf_op jit(solution)/shard_map/rows/pallas_call | solution.py:518
  125.0 0.8 reduce.3
  125.8 0.6 copy.14
  (1 shorter events, 0.0 us)
Async XLA Ops:
  4.0 0.7 copy-start
  4.7 0.7 copy-start.1

commit v3 on v2

--- a/solution.py
+++ b/solution.py
@@ -10,19 +10,20 @@
 BLOCK = 256
 ITERS = 3
 FLOOR = -1e30
+SMALL = 1e-20
 GROUP = 16
 ROWS = 32
 AHEAD = 2
-CHUNKS = 2
+CHUNKS = 1
 EXTRA = 16
 HALVES = (pl.ds(0, BLOCK // 2), pl.ds(BLOCK // 2, BLOCK // 2))
 VMEM_BYTES = 50 * 1024 * 1024
 
 
-def scores_of(source_ref, gathered, which, slot, slots, lanes):
+def scores_of(source_ref, gathered, which, slot, slots):
     width = gathered.shape[1]
     source = source_ref[pl.ds(pl.multiple_of(which * BLOCK, BLOCK), BLOCK), pl.ds(0, width)]
-    targets = gathered[which * slots + slot, :, lanes]
+    targets = gathered[which * slots + slot]
     return jnp.dot(source, targets, preferred_element_type=jnp.float32)
 
 
@@ -88,15 +89,10 @@
         for k in range(GROUP):
             slot = lax.rem(group * GROUP, slots) + k
             row = row_of(columns_ref, counts_ref, which, slot, target_count)
-            top_parts = []
-            sum_parts = []
-            for lanes in HALVES:
-                scores = scores_of(source_ref, gathered, which, slot, slots, lanes)
-                top = jnp.max(scores, axis=0, keepdims=True)
-                top_parts.append(top)
-                sum_parts.append(jnp.sum(jnp.exp(scores - top), axis=0, keepdims=True))
-            tops[which, pl.ds(row, 1), :] = jnp.concatenate(top_parts, axis=1)
-            sums[which, pl.ds(row, 1), :] = jnp.concatenate(sum_parts, axis=1)
+            scores = scores_of(source_ref, gathered, which, slot, slots)
+            top = jnp.max(scores, axis=0, keepdims=True)
+            tops[which, pl.ds(row, 1), :] = top
+            sums[which, pl.ds(row, 1), :] = jnp.sum(jnp.exp(scores - top), axis=0, keepdims=True)
 
     def ahead(group, _):
         start(group + AHEAD)
@@ -144,9 +140,9 @@
     *rest,
 ):
     if columns_out:
-        out_ref, held, partial, source, dense = rest
+        out_ref, partial, source, shift, held, dense = rest
     else:
-        own_ref, partial, source = rest
+        own_ref, partial, source, shift = rest
     own, slots = columns_ref.shape
     target_count = pot_ref.shape[0]
     if columns_out:
@@ -175,26 +171,6 @@
             targets = jnp.concatenate([gathered[which * slots + slot], extra], axis=0)
             return jnp.dot(source[...], targets, preferred_element_type=jnp.float32)
 
-        if first:
-            set_source(jnp.zeros((BLOCK, 1), jnp.float32))
-            partial[...] = jnp.full(partial.shape, FLOOR, jnp.float32)
-
-            def top_group(i, _):
-                best = partial[...]
-                for k in range(GROUP):
-                    low, high = halves(shifted(i * GROUP + k))
-                    best = jnp.maximum(best, jnp.maximum(low, high))
-                partial[...] = best
-                return 0
-
-            lax.fori_loop(0, groups, top_group, 0)
-            offset = -jnp.max(partial[...], axis=1, keepdims=True)
-        else:
-            offset = old_ref[own_rows, :]
-
-        set_source(offset)
-        partial[...] = jnp.zeros(partial.shape, jnp.float32)
-
         def sum_group(i, _):
             total = partial[...]
             for k in range(GROUP):
@@ -207,7 +183,33 @@
             partial[...] = total
             return 0
 
-        lax.fori_loop(0, groups, sum_group, 0)
+        def sum_all(offset):
+            shift[...] = offset
+            set_source(offset)
+            partial[...] = jnp.zeros(partial.shape, jnp.float32)
+            lax.fori_loop(0, groups, sum_group, 0)
+
+        if first:
+            sum_all(jnp.zeros((BLOCK, 1), jnp.float32))
+
+            @pl.when(jnp.min(jnp.sum(partial[...], axis=1, keepdims=True)) < SMALL)
+            def _():
+                set_source(jnp.zeros((BLOCK, 1), jnp.float32))
+                partial[...] = jnp.full(partial.shape, FLOOR, jnp.float32)
+
+                def top_group(i, _):
+                    best = partial[...]
+                    for k in range(GROUP):
+                        low, high = halves(shifted(i * GROUP + k))
+                        best = jnp.maximum(best, jnp.maximum(low, high))
+                    partial[...] = best
+                    return 0
+
+                lax.fori_loop(0, groups, top_group, 0)
+                sum_all(-jnp.max(partial[...], axis=1, keepdims=True))
+        else:
+            sum_all(old_ref[own_rows, :])
+        offset = shift[...]
         total = jnp.sum(partial[...], axis=1, keepdims=True)
         weights = weights_ref[own_rows, :]
         new_ref[own_rows, :] = weights + offset - jnp.log(total)
@@ -245,6 +247,9 @@
 
 
 def stages_of(devices):
+    if devices % 16 == 0:
+        out = [(2, 1), (8, 2)]
+        return out if devices == 16 else out + [(devices // 16, 16)]
     radices = []
     rest = devices
     if rest % 2 == 0:
@@ -474,13 +479,14 @@
     def rows(first, columns_out):
         partial = pltpu.VMEM((BLOCK, BLOCK // 2), jnp.float32)
         source = pltpu.VMEM((BLOCK, width + EXTRA), source_features.dtype)
+        shift = pltpu.VMEM((BLOCK, 1), jnp.float32)
         held = pltpu.VMEM((slots, BLOCK, BLOCK), jnp.float32)
         return pl.pallas_call(
             functools.partial(rows_kernel, first, columns_out),
             out_shape=(per_source, whole if columns_out else part),
             in_specs=[in_smem, in_smem, in_vmem, in_vmem, in_vmem, in_vmem, in_vmem],
             out_specs=(in_vmem, in_vmem),
-            scratch_shapes=[held, partial, source, dense] if columns_out else [partial, source],
+            scratch_shapes=[partial, source, shift] + ([held, dense] if columns_out else []),
             compiler_params=params,
             name="rows",
         )

time: 127 us -> 120 us (0.945)
  Pallas kernels: 120 us -> 113 us
    pallas_call x3, Pallas kernels: 39.4 us -> 33.8 us  [local(): rows(sweep == 0, not last)]
    pallas_call x1, Pallas kernels: 22.9 us -> 21.5 us  [local(): target_pot = reduce_call(True)(term, weights_tgt, weights_tgt)]
where the time goes in v3:
time: 120 us; the launch traced here: 119 us
  Pallas kernels  113 us (94%)
  local copies, waits for them, and re-layouts  5.22 us (4%)
    pallas_call x2, Pallas kernels, local(): target_pot = reduce_call(False)(term, weights_tgt, target_pot)  41.5 us
    pallas_call x3, Pallas kernels, local(): rows(sweep == 0, not last)  33.8 us
    pallas_call x1, Pallas kernels, local(): target_pot = reduce_call(True)(term, weights_tgt, weights_tgt)  21.5 us
    pallas_call x1, Pallas kernels, local(): term, picked = first_term(block_columns, block_counts, sources, targets)  15.7 us
    unnamed x6, local copies, waits for them, and re-layouts  3.03 us

profile of v3, /device:TPU:0, one launch (start us, length us, event | category | flops | bytes accessed | tf_op | source)
XLA Modules:
  0.0 119.4 jit_solution(8298523501701527702)
XLA Ops:
  0.6 0.1 pad.1.clone
  0.7 1.1 copy.9
  1.8 0.1 pad_maximum_fusion.source_ref
  1.9 0.9 copy.13.weights_ref.old_ref
  2.8 1.2 %reshape.17.weights_ref.old_ref = f32[512,256]{1,0:T(8,128)S(1)} reshape(f32[131072]{0:T(1024)} %param.9) | data formatting | bytes 1048576 | tf_op jit(solution)/shard_map/reshape | solution.py:454
  4.0 0.0 copy-start
  4.0 0.7 copy-done
  4.7 0.0 copy-start.1
  4.7 0.7 copy-done.1
  5.3 15.7 %first_columns.1 = (f32[512,256]{1,0:T(8,128)S(1)}, bf16[128,64,256]{2,1,0:T(8,128)(2,1)}) custom-call(s32[4,32]{1,0:T(4,128)S(1)} %copy-done, s32[4]{0:T(128)S(1)} %copy-done.1, bf16[1024,80]{1,0:T(8,128)(2,1)S(1)} %pad_maximum_fusion.source_ref, bf16[64,131072]{1,0:T(8,128)(2,1)} %bitcast.5), custom_call_target="tpu_custom_call" | custom-call | tf_op jit(solution)/shard_map/first_columns/pallas_call | solution.py:519
  21.1 21.5 %reduce.4.pot_ref.old_ref = f32[512,256]{1,0:T(8,128)S(1)} custom-call(f32[512,256]{1,0:T(8,128)S(1)} %get-tuple-element.10.term_ref, f32[512,256]{1,0:T(8,128)S(1)} %reshape.17.weights_ref.old_ref, f32[512,256]{1,0:T(8,128)S(1)} %reshape.17.weights_ref.old_ref), custom_call_target="tpu_custom_call" | custom-call | tf_op jit(solution)/shard_map/reduce/pallas_call | solution.py:520
  42.6 12.6 %rows.3 = (f32[1024,1]{1,0:T(8,128)S(1)}, f32[512,256]{1,0:T(8,128)S(1)}) custom-call(s32[4,32]{1,0:T(4,128)S(1)} %copy-done, s32[4]{0:T(128)S(1)} %copy-done.1, bf16[1024,80]{1,0:T(8,128)(2,1)S(1)} %pad_maximum_fusion.source_ref, f32[1024,1]{1,0:T(8,128)S(1)} %copy.13.weights_ref.old_ref, f32[1024,1]{1,0:T(8,128)S(1)} %copy.13.weights_ref.old_ref, ...), custom_call_target="tpu_custom_call" | custom-call | tf_op jit(solution)/shard_map/rows/pallas_call | solution.py:524
  55.2 20.8 %reduce.5.pot_ref.old_ref = f32[512,256]{1,0:T(8,128)S(1)} custom-call(f32[512,256]{1,0:T(8,128)S(1)} %get-tuple-element.13.term_ref, f32[512,256]{1,0:T(8,128)S(1)} %reshape.17.weights_ref.old_ref, f32[512,256]{1,0:T(8,128)S(1)} %reduce.4.pot_ref.old_ref), custom_call_target="tpu_custom_call" | custom-call | tf_op jit(solution)/shard_map/reduce/pallas_call | solution.py:528
  76.0 12.3 %rows.4 = (f32[1024,1]{1,0:T(8,128)S(1)}, f32[512,256]{1,0:T(8,128)S(1)}) custom-call(s32[4,32]{1,0:T(4,128)S(1)} %copy-done, s32[4]{0:T(128)S(1)} %copy-done.1, bf16[1024,80]{1,0:T(8,128)(2,1)S(1)} %pad_maximum_fusion.source_ref, f32[1024,1]{1,0:T(8,128)S(1)} %copy.13.weights_ref.old_ref, f32[1024,1]{1,0:T(8,128)S(1)} %get-tuple-element.12.old_ref, ...), custom_call_target="tpu_custom_call" | custom-call | tf_op jit(solution)/shard_map/rows/pallas_call | solution.py:524
  88.3 20.7 %reduce.6.pot_ref = f32[512,256]{1,0:T(8,128)S(1)} custom-call(f32[512,256]{1,0:T(8,128)S(1)} %get-tuple-element.15.term_ref, f32[512,256]{1,0:T(8,128)S(1)} %reshape.17.weights_ref.old_ref, f32[512,256]{1,0:T(8,128)S(1)} %reduce.5.pot_ref.old_ref), custom_call_target="tpu_custom_call" | custom-call | tf_op jit(solution)/shard_map/reduce/pallas_call | solution.py:528
  109.0 8.9 %rows.5 = (f32[1024,1]{1,0:T(8,128)S(1)}, f32[32,256]{1,0:T(8,128)S(1)}) custom-call(s32[4,32]{1,0:T(4,128)S(1)} %copy-done, s32[4]{0:T(128)S(1)} %copy-done.1, bf16[1024,80]{1,0:T(8,128)(2,1)S(1)} %pad_maximum_fusion.source_ref, f32[1024,1]{1,0:T(8,128)S(1)} %copy.13.weights_ref.old_ref, f32[1024,1]{1,0:T(8,128)S(1)} %get-tuple-element.14.old_ref, ...), custom_call_target="tpu_custom_call" | custom-call | tf_op jit(solution)/shard_map/rows/pallas_call | solution.py:524
  117.9 0.8 reduce.3
  118.7 0.6 copy.14
  (1 shorter events, 0.0 us)
Async XLA Ops:
  4.0 0.7 copy-start
  4.7 0.7 copy-start.1
